TPU v7x, 32 devices: a whole 2x2x4 slice. The times are simulated.
32 devices in a mesh: parts: 2 (over x), seq: 16 (over z, y, core).
Axes of the slice: x: 2, y: 2, z: 4, core: 2. Of those that a mesh axis runs over, the one named last changes fastest.
Arguments:
- inputs: bfloat16 [524288, 512], P(('parts', 'seq')), parts along dimension 0, may hold values from -6 to 6
- cotangent: bfloat16 [524288, 512], P(('parts', 'seq')), parts along dimension 0, may hold values from -6 to 6
- first_block: bfloat16 [512, 512], P('seq'), may hold values from -0.25 to 0.25
- second_block: bfloat16 [512, 512], P('seq'), may hold values from -0.25 to 0.25
- twiddle: float32 [512, 512], P('seq'), may hold values from 0.25 to 1.75
Outputs:
- grad_input: bfloat16 [524288, 512], P(('parts', 'seq')), parts along dimension 0
- grad_first: float32 [1024, 512], P(('parts', 'seq')), parts along dimension 0
- grad_second: float32 [1024, 512], P(('parts', 'seq')), parts along dimension 0
- grad_twiddle: float32 [1024, 512], P(('parts', 'seq')), parts along dimension 0
There are 2 independent parts, one for each index of `parts`. A program takes and returns all parts, laid end to end along the dimension named above; an argument that names none is the same for every part. Nothing has to cross between parts.
All inputs are finite; a program needn't handle non-finite values.
Results may differ from a plain program's by a relative error of at most 0.0061.
Values may be sent and summed in bfloat16 or wider, within the bound.
A program may use at most 320 MiB of HBM per device.

v0:
```python
import jax
import jax.numpy as jnp
from jax import lax
from jax.sharding import PartitionSpec as P


def forward_inner(block_two, tw_cols, mixed_rows):
    scaled = (tw_cols * mixed_rows.astype(jnp.float32)).astype(jnp.bfloat16)
    gated_rows = jnp.einsum(
        "ik,kjc->ijc", block_two, scaled, preferred_element_type=jnp.float32
    ).astype(jnp.bfloat16)
    return (scaled, gated_rows)


def backward_inner(block_two, tw_cols, grad_rows, mixed_rows, channels):
    back_two = jnp.einsum("ki,kjc->ijc", block_two, grad_rows, preferred_element_type=jnp.float32)
    tw_grad = jnp.sum(back_two * mixed_rows.astype(jnp.float32), axis=2).T / channels**0.5
    back_one = (tw_cols * back_two).astype(jnp.bfloat16)
    return (tw_grad, back_one)


def on_device(inputs, cotangent, first_block, second_block, twiddle):
    channels = inputs.shape[1]
    order = first_block.shape[1]
    local_blocks = inputs.shape[0] // order
    xval = inputs.reshape(local_blocks, order, channels)
    dyval = cotangent.reshape(local_blocks, order, channels)
    block_one, block_two = (
        lax.all_gather(first_block, "seq", axis=0, tiled=True),
        lax.all_gather(second_block, "seq", axis=0, tiled=True),
    )
    tw_cols = twiddle.T[:, :, None]
    mixed_one = jnp.einsum(
        "jk,ikc->ijc", block_one, xval, preferred_element_type=jnp.float32
    ).astype(jnp.bfloat16)
    grad_mix = (dyval.astype(jnp.float32) * xval.astype(jnp.float32)).astype(jnp.bfloat16)
    mixed_rows, grad_rows = (
        lax.all_to_all(mixed_one, "seq", split_axis=1, concat_axis=0, tiled=True),
        lax.all_to_all(grad_mix, "seq", split_axis=1, concat_axis=0, tiled=True),
    )
    scaled, gated_rows = forward_inner(block_two, tw_cols, mixed_rows)
    tw_grad, back_rows = backward_inner(block_two, tw_cols, grad_rows, mixed_rows, channels)
    gated_mix, back_one = (
        lax.all_to_all(gated_rows, "seq", split_axis=0, concat_axis=1, tiled=True),
        lax.all_to_all(back_rows, "seq", split_axis=0, concat_axis=1, tiled=True),
    )
    second_term = (
        jnp.einsum("ijc,kjc->ik", grad_rows, scaled, preferred_element_type=jnp.float32) / channels
    )
    grad_second = lax.psum_scatter(second_term, "seq", scatter_dimension=0, tiled=True)
    first_term = (
        jnp.einsum("ijc,ikc->jk", back_one, xval, preferred_element_type=jnp.float32) / channels
    )
    grad_first = lax.psum_scatter(first_term, "seq", scatter_dimension=0, tiled=True)
    total = dyval.astype(jnp.float32) * gated_mix.astype(jnp.float32)
    total = total + jnp.einsum(
        "jk,ijc->ikc", block_one, back_one, preferred_element_type=jnp.float32
    )
    grad_input = total.astype(jnp.bfloat16).reshape(local_blocks * order, channels)
    return (grad_input, grad_first, grad_second, tw_grad)


def solution(mesh):
    in_specs = (
        P(("parts", "seq"), None),
        P(("parts", "seq"), None),
        P("seq", None),
        P("seq", None),
        P("seq", None),
    )
    out_specs = (
        P(("parts", "seq"), None),
        P(("parts", "seq"), None),
        P(("parts", "seq"), None),
        P(("parts", "seq"), None),
    )
    return jax.shard_map(
        on_device, mesh=mesh, in_specs=in_specs, out_specs=out_specs, check_vma=False
    )
```

profile of v0, /device:TPU:15, one launch (start us, length us, event | category | flops | bytes accessed | tf_op | source)
XLA Modules:
  0.0 1785.7 jit_solution(997493110390584822)
XLA Ops:
  7.2 17.3 all_gather.6
  24.5 0.0 copy-start
  24.5 18.6 %convert_bitcast_fusion.3 = bf16[32,512,512]{1,2,0:T(8,128)(2,1)} fusion(bf16[32,512,512]{2,1,0:T(8,128)(2,1)} %bitcast.70, bf16[512,512]{1,0:T(8,128)(2,1)S(1)} %all_gather.6), kind=kOutput, calls=%fused_computation.13 | convolution fusion | flops 8598323200 | bytes 34078720 | tf_op jit(solution)/shard_map/jk,ikc->ijc/dot_general | solution.py:33
  43.0 0.0 copy-done
  43.0 28.6 %copy.44 = bf16[32,512,512]{2,0,1:T(8,128)(2,1)} copy(bf16[32,512,512]{1,2,0:T(8,128)(2,1)} %convert_bitcast_fusion.3) | data formatting | bytes 33554432 | tf_op jit(solution)/shard_map/convert_element_type | solution.py:35
  71.6 11.7 all-to-all-start
  83.3 13.3 fusion.2
  96.6 26.6 %copy.50 = bf16[32,512,512]{2,0,1:T(8,128)(2,1)} copy(bf16[32,512,512]{2,1,0:T(8,128)(2,1)S(1)} %fusion.2) | data formatting | bytes 33554432 | tf_op jit(solution)/shard_map/convert_element_type | solution.py:36
  123.3 0.0 copy-start.3
  123.3 322.2 %all-to-all-done = bf16[32,512,512]{2,0,1:T(8,128)(2,1)} async-done(((bf16[32,512,512]{2,0,1:T(8,128)(2,1)}), bf16[32,512,512]{2,0,1:T(8,128)(2,1)}, u32[]{:S(2)}, u32[]{:S(2)}) %all-to-all-start) | async-done | bytes 16777248 | tf_op jit(solution)/shard_map/all_to_all | solution.py:38
  445.5 5.0 all-to-all-start.2
  450.5 0.0 copy-done.3
  450.5 373.4 %all_gather.7 = bf16[512,512]{1,0:T(8,128)(2,1)S(1)} all-gather(bf16[32,512]{1,0:T(8,128)(2,1)S(1)} %copy-done.3), channel_id=1, replica_groups=mesh['parts'=2,'seq'=16] {'seq'}, dimensions={0}, use_global_device_ids=true | all-gather | bytes 557056 | tf_op jit(solution)/shard_map/all_gather | solution.py:30
  823.9 16.8 copy.45
  840.6 9.8 convert_bitcast_fusion.1
  850.5 11.9 copy.46
  862.4 0.0 copy-start.2
  862.4 38.0 %copy.47 = f32[512,32,512]{0,2,1:T(8,128)} copy(f32[512,32,512]{2,1,0:T(8,128)} %bitcast.63) | data formatting | bytes 67108864 | tf_op jit(solution)/shard_map/convert_element_type | solution.py:8
  900.4 0.0 copy-done.2
  900.4 21.2 %convert_bitcast_fusion.2 = bf16[512,32,512]{0,2,1:T(8,128)(2,1)} fusion(f32[512,32,512]{0,2,1:T(8,128)} %copy.47, f32[512,32]{0,1:T(8,128)S(1)} %bitcast.75, bf16[512,512]{1,0:T(8,128)(2,1)S(1)} %all_gather.7), kind=kOutput, calls=%fused_computation.12 | convolution fusion | flops 8615100416 | bytes 50921472 | tf_op jit(solution)/shard_map/ik,kjc->ijc/dot_general | solution.py:9
  921.6 28.6 %copy.48 = bf16[512,32,512]{2,1,0:T(8,128)(2,1)} copy(bf16[512,32,512]{0,2,1:T(8,128)(2,1)} %convert_bitcast_fusion.2) | data formatting | bytes 33554432 | tf_op jit(solution)/shard_map/convert_element_type | solution.py:11
  950.2 0.0 all-to-all-done.2
  950.2 5.3 all-to-all-start.1
  955.5 18.4 %copy.52 = bf16[16,32,32,512]{3,2,1,0:T(8,128)(2,1)} copy(bf16[16,32,32,512]{3,1,2,0:T(8,128)(2,1)} %bitcast.16) | data formatting | bytes 33554432 | tf_op jit(solution)/shard_map/all_to_all | solution.py:39
  974.0 28.9 %fusion.4 = (f32[512,32]{0,1:T(8,128)S(1)}, bf16[512,32,512]{0,2,1:T(8,128)(2,1)}) fusion(f32[512,32,512]{0,2,1:T(8,128)} %copy.47, f32[512,32]{0,1:T(8,128)S(1)} %bitcast.76, bf16[512,512]{1,0:T(8,128)(2,1)S(1)} %all_gather.7, bf16[512,32,512]{2,1,0:T(8,128)(2,1)} %bitcast.73), kind=kOutput, calls=%fused_computation.10 | convolution fusion | flops 8623472640 | bytes 67764224 | tf_op jit(solution)/shard_map/ki,kjc->ijc/dot_general | solution.py:16
  1002.9 28.6 %copy.54 = bf16[512,32,512]{2,1,0:T(8,128)(2,1)} copy(bf16[512,32,512]{0,2,1:T(8,128)(2,1)} %get-tuple-element.5) | data formatting | bytes 33554432 | tf_op jit(solution)/shard_map/convert_element_type | solution.py:18
  1031.5 286.9 %all-to-all-done.1 = bf16[512,32,512]{2,1,0:T(8,128)(2,1)} async-done(((bf16[512,32,512]{2,1,0:T(8,128)(2,1)}), bf16[512,32,512]{2,1,0:T(8,128)(2,1)}, u32[]{:S(2)}, u32[]{:S(2)}) %all-to-all-start.1) | async-done | bytes 16777248 | tf_op jit(solution)/shard_map/all_to_all | solution.py:44
  1318.4 5.0 all-to-all-start.3
  1323.4 0.0 reduce-scatter.5.cloned.1.call-start
  1323.5 23.2 %fusion.13 = f32[512,512]{1,0:T(8,128)} fusion(f32[512,32,512]{0,2,1:T(8,128)} %copy.47, f32[512,32]{0,1:T(8,128)S(1)} %bitcast.77, bf16[512,32,512]{2,1,0:T(8,128)(2,1)} %bitcast.74), kind=kOutput, calls=%fused_computation.21 | convolution fusion | flops 8606973952 | bytes 51445760 | tf_op jit(solution)/shard_map/ijc,kjc->ik/dot_general | solution.py:48
  1346.7 0.0 reduce-scatter.5.cloned.1.call-update
  1346.8 0.3 reduce-scatter.3.cloned.1.call-start
  1347.1 0.6 multiply_bitcast_fusion
  1347.7 9.9 convert_bitcast_fusion
  1357.6 11.9 copy.49
  1369.5 322.2 %all-to-all-done.3 = bf16[512,32,512]{2,1,0:T(8,128)(2,1)} async-done(((bf16[512,32,512]{2,1,0:T(8,128)(2,1)}), bf16[512,32,512]{2,1,0:T(8,128)(2,1)}, u32[]{:S(2)}, u32[]{:S(2)}) %all-to-all-start.3) | async-done | bytes 16777248 | tf_op jit(solution)/shard_map/all_to_all | solution.py:45
  1691.7 14.1 copy.55
  1705.8 0.0 copy-start.1
  1705.8 18.1 %fusion.9 = f32[512,512]{1,0:T(8,128)} fusion(bf16[32,512,512]{2,1,0:T(8,128)(2,1)} %bitcast.66, bf16[32,512,512]{2,1,0:T(8,128)(2,1)} %bitcast.72), kind=kOutput, calls=%fused_computation.19 | convolution fusion | flops 8590196736 | bytes 34603008 | tf_op jit(solution)/shard_map/ijc,ikc->jk/dot_general | solution.py:52
  1723.9 0.0 reduce-scatter.3.cloned.1.call-update
  1723.9 0.0 copy-done.1
  1723.9 30.2 %fusion.1 = bf16[32,512,512]{2,1,0:T(8,128)(2,1)} fusion(bf16[32,512,512]{2,1,0:T(8,128)(2,1)} %bitcast.65, f32[32,16,32,512]{3,2,1,0:T(8,128)} %copy.49, bf16[32,512,512]{2,1,0:T(8,128)(2,1)} %bitcast.67, bf16[512,512]{1,0:T(8,128)(2,1)S(1)} %copy-done.1), kind=kOutput, calls=%fused_computation.3 | convolution fusion | flops 8623489024 | bytes 84410368 | tf_op jit(solution)/shard_map/jk,ijc->ikc/dot_general | solution.py:56
  1754.1 0.0 reduce-scatter.5.cloned.1.call-done
  1754.1 24.8 %reduce-scatter.3.cloned.1.call-done = f32[32,512]{1,0:T(8,128)} async-done(((f32[512,512]{1,0:T(8,128)}), f32[32,512]{1,0:T(8,128)}) %reduce-scatter.3.cloned.1.call-update) | async-done | bytes 65552 | tf_op jit(solution)/shard_map/reduce_scatter | solution.py:54
Async XLA Ops:
  24.5 18.6 %copy-start = (bf16[512,512]{1,0:T(8,128)(2,1)}, bf16[512,512]{1,0:T(8,128)(2,1)S(1)}, u32[]{:S(2)}) copy-start(bf16[512,512]{1,0:T(8,128)(2,1)S(1)} %all_gather.6) | copy-start | bytes 1572868
  71.6 373.8 %all-to-all-start = ((bf16[32,512,512]{2,0,1:T(8,128)(2,1)}), bf16[32,512,512]{2,0,1:T(8,128)(2,1)}, u32[]{:S(2)}, u32[]{:S(2)}) async-start(bf16[32,512,512]{2,0,1:T(8,128)(2,1)} %copy.44), calls=%async_computation | async-start | bytes 33554432 | tf_op jit(solution)/shard_map/all_to_all | solution.py:38
  123.3 327.2 %copy-start.3 = (bf16[32,512]{1,0:T(8,128)(2,1)S(1)}, bf16[32,512]{1,0:T(8,128)(2,1)}, u32[]{:S(2)}) copy-start(bf16[32,512]{1,0:T(8,128)(2,1)} %param.8) | copy-start | bytes 98308
  445.5 504.8 %all-to-all-start.2 = ((bf16[32,512,512]{2,0,1:T(8,128)(2,1)}), bf16[32,512,512]{2,0,1:T(8,128)(2,1)}, u32[]{:S(2)}, u32[]{:S(2)}) async-start(bf16[32,512,512]{2,0,1:T(8,128)(2,1)} %copy.50), calls=%async_computation.2 | async-start | bytes 33554432 | tf_op jit(solution)/shard_map/all_to_all | solution.py:39
  862.4 38.0 %copy-start.2 = (f32[32,512]{1,0:T(8,128)S(1)}, f32[32,512]{1,0:T(8,128)}, u32[]{:S(2)}) copy-start(f32[32,512]{1,0:T(8,128)} %param.9) | copy-start | bytes 196612
  950.2 368.2 %all-to-all-start.1 = ((bf16[512,32,512]{2,1,0:T(8,128)(2,1)}), bf16[512,32,512]{2,1,0:T(8,128)(2,1)}, u32[]{:S(2)}, u32[]{:S(2)}) async-start(bf16[512,32,512]{2,1,0:T(8,128)(2,1)} %copy.48), calls=%async_computation.1 | async-start | bytes 33554432 | tf_op jit(solution)/shard_map/all_to_all | solution.py:44
  1318.4 373.3 %all-to-all-start.3 = ((bf16[512,32,512]{2,1,0:T(8,128)(2,1)}), bf16[512,32,512]{2,1,0:T(8,128)(2,1)}, u32[]{:S(2)}, u32[]{:S(2)}) async-start(bf16[512,32,512]{2,1,0:T(8,128)(2,1)} %copy.54), calls=%async_computation.3 | async-start | bytes 33554432 | tf_op jit(solution)/shard_map/all_to_all | solution.py:45
  1323.4 430.7 %reduce-scatter.5.cloned.1.call-start = ((), (), s32[]{:S(2)}) async-start(), calls=%async_computation.7 | async-start | bytes 1114112 | tf_op jit(solution)/shard_map/reduce_scatter | solution.py:50
  1346.8 432.1 %reduce-scatter.3.cloned.1.call-start = ((), (), s32[]{:S(2)}) async-start(), calls=%async_computation.6 | async-start | bytes 1114112 | tf_op jit(solution)/shard_map/reduce_scatter | solution.py:54
  1705.8 18.1 %copy-start.1 = (bf16[512,512]{1,0:T(8,128)(2,1)S(1)}, bf16[512,512]{1,0:T(8,128)(2,1)}, u32[]{:S(2)}) copy-start(bf16[512,512]{1,0:T(8,128)(2,1)} %copy-done) | copy-start | bytes 1572868
Sparse Core Ops, SparseCore 0:
  1346.9 237.7 reduce-scatter.4
  1724.0 54.8 reduce-scatter.2
where the time goes:
time: 1790 us
  waiting for transfers between devices  956 us (53%)
  blocking collectives  391 us (22%)
  local copies, waits for them, and re-layouts  224 us (13%)
  matrix products  140 us (8%)
  other arithmetic  33.6 us (2%)
  starting transfers between devices  27.4 us (2%)
    all_gather x1, blocking collectives, on_device(): lax.all_gather(second_block, 'seq', axis=0, tiled=True)  373 us
    all_to_all x1, waiting for transfers between devices, on_device(): lax.all_to_all(mixed_one, 'seq', split_axis=1, concat_axis=0, tiled=True)  322 us
    all_to_all x1, waiting for transfers between devices, on_device(): lax.all_to_all(back_rows, 'seq', split_axis=0, concat_axis=1, tiled=True)  322 us
    all_to_all x1, waiting for transfers between devices, on_device(): lax.all_to_all(gated_rows, 'seq', split_axis=0, concat_axis=1, tiled=True)  287 us
    convert_element_type x2, local copies, waits for them, and re-layouts, forward_inner(): scaled = (tw_cols * mixed_rows.astype(jnp.float32)).astype(jnp.bfloat16)  49.9 us
  transfers between devices with their start and end apart: 6, of which 4 were waited for; matrix products, arithmetic and copies ran while one was open for 20% of the time, Pallas kernels for 0%

commit v1 on v0

v1 whole, which is shorter than its diff:
```python
import jax
import jax.numpy as jnp
from jax import lax
from jax.experimental import pallas as pl
from jax.experimental.pallas import tpu as pltpu
from jax.sharding import PartitionSpec as P

F32 = jnp.float32
BF16 = jnp.bfloat16
LANES = 128


def channel_kernel(
    x_ref, dy_ref, f_ref, ft_ref, s_ref, st_ref, tw_ref, gf_in, gs_in, gt_in,
    gi_ref, gf_ref, gs_ref, gt_ref,
):
    @pl.when(pl.program_id(0) == 0)
    def _():
        gf_ref[...] = gf_in[...]
        gs_ref[...] = gs_in[...]
        gt_ref[...] = gt_in[...]

    order = f_ref.shape[0]
    xf = x_ref[...].astype(F32).reshape(order, order)
    dyf = dy_ref[...].astype(F32).reshape(order, order)
    xb = xf.astype(BF16)
    tw = tw_ref[...]
    m1 = jnp.dot(xb, ft_ref[...], preferred_element_type=F32).astype(BF16).astype(F32)
    scaled = (tw * m1).astype(BF16)
    grad_mix = (dyf * xf).astype(BF16)
    gated = jnp.dot(s_ref[...], scaled, preferred_element_type=F32).astype(BF16)
    back_two = jnp.dot(st_ref[...], grad_mix, preferred_element_type=F32)
    gt_ref[...] += back_two * m1
    back_one = (tw * back_two).astype(BF16)
    gs_ref[...] += lax.dot_general(
        grad_mix, scaled, (((1,), (1,)), ((), ())), preferred_element_type=F32
    )
    gf_ref[...] += lax.dot_general(
        back_one, xb, (((0,), (0,)), ((), ())), preferred_element_type=F32
    )
    gi = dyf * gated.astype(F32) + jnp.dot(back_one, f_ref[...], preferred_element_type=F32)
    gi_ref[...] = gi.reshape(gi_ref.shape).astype(BF16)


def channels_call(xc, dyc, f, ft, s, st, tw, grads):
    devices, own, rows, order = xc.shape
    block = pl.BlockSpec((devices, None, rows, order), lambda c: (0, c, 0, 0))
    square = pl.BlockSpec((order, order), lambda c: (0, 0))
    total = jax.ShapeDtypeStruct((order, order), F32)
    gi, *grads = pl.pallas_call(
        channel_kernel,
        grid=(own,),
        out_shape=(jax.ShapeDtypeStruct(xc.shape, BF16), total, total, total),
        in_specs=[block] * 2 + [square] * 8,
        out_specs=(block, square, square, square),
        compiler_params=pltpu.CompilerParams(vmem_limit_bytes=56 * 1024 * 1024),
        cost_estimate=pl.CostEstimate(
            flops=12 * own * order**3,
            bytes_accessed=6 * own * order**2 + 30 * order**2,
            transcendentals=0,
        ),
    )(xc, dyc, f, ft, s, st, tw, *grads)
    return gi, tuple(grads)


def to_channels_kernel(x_ref, o_ref, held):
    count = x_ref.shape[0]
    lanes = x_ref.shape[2]
    for i in range(count):
        for q in range(x_ref.shape[1] // LANES):
            square = x_ref[i, pl.ds(q * LANES, LANES), :].astype(F32).T
            held[pl.ds(q * lanes * count + i, lanes, stride=count), :] = square
    for q in range(x_ref.shape[1] // LANES):
        piece = held[pl.ds(q * lanes * count, lanes * count), :]
        o_ref[:, :, pl.ds(q * LANES, LANES)] = piece.reshape(lanes, count, LANES).astype(BF16)


def to_channels(array, at, chunk):
    rows, order, _ = array.shape
    count = min(rows, 16)
    return pl.pallas_call(
        to_channels_kernel,
        grid=(chunk // LANES, rows // count),
        out_shape=jax.ShapeDtypeStruct((chunk, rows, order), BF16),
        in_specs=[pl.BlockSpec((count, order, LANES), lambda c, i: (i, 0, at // LANES + c))],
        out_specs=pl.BlockSpec((LANES, count, order), lambda c, i: (c, i, 0)),
        scratch_shapes=[pltpu.VMEM((count * order, LANES), F32)],
        compiler_params=pltpu.CompilerParams(vmem_limit_bytes=56 * 1024 * 1024),
        cost_estimate=pl.CostEstimate(
            flops=0, bytes_accessed=4 * chunk * rows * order, transcendentals=0
        ),
    )(array)


def to_positions_kernel(b_ref, *refs):
    o_ref, held = refs[-2:]
    count = o_ref.shape[0]
    lanes = o_ref.shape[2]
    for q in range(o_ref.shape[1] // LANES):
        piece = b_ref[:, :, pl.ds(q * LANES, LANES)].astype(F32)
        held[pl.ds(q * lanes * count, lanes * count), :] = piece.reshape(lanes * count, LANES)
    for i in range(count):
        for q in range(o_ref.shape[1] // LANES):
            square = held[pl.ds(q * lanes * count + i, lanes, stride=count), :].T
            o_ref[i, pl.ds(q * LANES, LANES), :] = square.astype(BF16)


def to_positions(back, at, channels, result):
    chunk, rows, order = back.shape
    count = min(rows, 16)
    return pl.pallas_call(
        to_positions_kernel,
        grid=(chunk // LANES, rows // count),
        out_shape=jax.ShapeDtypeStruct((rows, order, channels), BF16),
        in_specs=[pl.BlockSpec((LANES, count, order), lambda c, i: (c, i, 0))]
        + [pl.BlockSpec(memory_space=pl.ANY)] * len(result),
        out_specs=pl.BlockSpec((count, order, LANES), lambda c, i: (i, 0, at // LANES + c)),
        scratch_shapes=[pltpu.VMEM((count * order, LANES), F32)],
        input_output_aliases={1: 0} if result else {},
        compiler_params=pltpu.CompilerParams(vmem_limit_bytes=56 * 1024 * 1024),
        cost_estimate=pl.CostEstimate(
            flops=0, bytes_accessed=4 * chunk * rows * order, transcendentals=0
        ),
    )(back, *result)


def on_device(inputs, cotangent, first_block, second_block, twiddle):
    channels = inputs.shape[1]
    rows, order = first_block.shape
    devices = order // rows
    chunk = channels // 2
    own = chunk // devices
    xval = inputs.reshape(rows, order, channels)
    dyval = cotangent.reshape(rows, order, channels)

    def send(array, at):
        part = to_channels(array, at, chunk).reshape(devices, own, rows, order)
        return lax.all_to_all(part, "seq", split_axis=0, concat_axis=0)

    small = jnp.stack([first_block.astype(F32), second_block.astype(F32), twiddle])
    small = lax.all_gather(small, "seq", axis=0)
    small = small.transpose(1, 0, 2, 3).reshape(3, order, order)
    f, s = small[0].astype(BF16), small[1].astype(BF16)
    ft, st, tw = f.T, s.T, small[2].T

    zero = jnp.zeros((order, order), F32)
    grads = (zero, zero, zero)
    result = ()
    for at in range(0, channels, chunk):
        gi, grads = channels_call(send(xval, at), send(dyval, at), f, ft, s, st, tw, grads)
        back = lax.all_to_all(gi, "seq", split_axis=0, concat_axis=0)
        result = (to_positions(back.reshape(chunk, rows, order), at, channels, result),)

    first, second, tw_grad = grads
    terms = jnp.stack([first, second, tw_grad.T]).reshape(3, devices, rows, order)
    terms = terms.transpose(1, 0, 2, 3).reshape(3 * order, order)
    terms = lax.psum_scatter(terms, "seq", scatter_dimension=0, tiled=True)
    terms = terms.reshape(3, rows, order)
    grad_first = terms[0] / channels
    grad_second = terms[1] / channels
    grad_twiddle = terms[2] / channels**0.5
    return (result[0].reshape(rows * order, channels), grad_first, grad_second, grad_twiddle)


def solution(mesh):
    in_specs = (
        P(("parts", "seq"), None),
        P(("parts", "seq"), None),
        P("seq", None),
        P("seq", None),
        P("seq", None),
    )
    out_specs = (
        P(("parts", "seq"), None),
        P(("parts", "seq"), None),
        P(("parts", "seq"), None),
        P(("parts", "seq"), None),
    )
    return jax.shard_map(
        on_device, mesh=mesh, in_specs=in_specs, out_specs=out_specs, check_vma=False
    )
```

time: 1790 us -> 1210 us (0.68)
  blocking collectives: 391 us -> 0 us
  local copies, waits for them, and re-layouts: 224 us -> 8.34 us
  Pallas kernels: 0 us -> 151 us
  matrix products: 140 us -> 0 us
  waiting for transfers between devices: 956 us -> 992 us
  other arithmetic: 33.6 us -> 5.94 us
    all_gather x2 -> x0, blocking collectives: 391 us -> none  [the longest x1 373 us: on_device(): lax.all_gather(second_block, 'seq', axis=0, tiled=True)]
    all_to_all x4 -> x6, waiting for transfers between devices: 931 us -> 679 us  [the longest x4 509 us: send(): return lax.all_to_all(part, 'seq', split_axis=0, concat_axis=0)]
    convert_element_type x7 -> x2, local copies, waits for them, and re-layouts: 174 us -> 2.14 us  [on_device(): f, s = (small[0].astype(BF16), small[1].astype(BF16))]
    all_gather x0 -> x1, waiting for transfers between devices: none -> 154 us  [on_device(): small = lax.all_gather(small, 'seq', axis=0)]
    pallas_call x0 -> x8, Pallas kernels: none -> 151 us  [the longest x2 74.6 us: channels_call(): pl.pallas_call(channel_kernel, grid=(own,), out_shape=(jax.ShapeDtypeStru...]
    dot_general x6 -> x0, matrix products: 140 us -> none  [the longest x1 30.2 us: on_device(): jnp.einsum('jk,ijc->ikc', block_one, back_one, preferred_element_type=jnp...]
    reduce_scatter x2 -> x1, waiting for transfers between devices: 24.8 us -> 158 us  [on_device(): terms = lax.psum_scatter(terms, 'seq', scatter_dimension=0, tiled=True)]
    all_to_all x3 -> x0, local copies, waits for them, and re-layouts: 49.3 us -> none  [the longest x1 18.4 us: on_device(): lax.all_to_all(grad_mix, 'seq', split_axis=1, concat_axis=0, tiled=True)]
  transfers between devices with their start and end apart: 6 -> 8, of which waited for: 4 -> 8; matrix products, arithmetic and copies ran while one was open for 20% -> 1% of each run, Pallas kernels for 0% -> 10%
where the time goes in v1:
time: 1210 us
  waiting for transfers between devices  992 us (82%)
  Pallas kernels  151 us (12%)
  starting transfers between devices  36.8 us (3%)
  between operations  14.2 us (1%)
    all_to_all x4, waiting for transfers between devices, send(): return lax.all_to_all(part, 'seq', split_axis=0, concat_axis=0)  509 us
    all_to_all x2, waiting for transfers between devices, on_device(): back = lax.all_to_all(gi, 'seq', split_axis=0, concat_axis=0)  170 us
    reduce_scatter x1, waiting for transfers between devices, on_device(): terms = lax.psum_scatter(terms, 'seq', scatter_dimension=0, tiled=True)  158 us
    all_gather x1, waiting for transfers between devices, on_device(): small = lax.all_gather(small, 'seq', axis=0)  154 us
    pallas_call x2, Pallas kernels, channels_call(): pl.pallas_call(channel_kernel, grid=(own,), out_shape=(jax.ShapeDtypeStru...  74.6 us
    pallas_call x4, Pallas kernels, to_channels(): pl.pallas_call(to_channels_kernel, grid=(chunk // LANES, rows // count),...  52.3 us
  transfers between devices with their start and end apart: 8, of which 8 were waited for; matrix products, arithmetic and copies ran while one was open for 1% of the time, Pallas kernels for 10%

profile of v1, /device:TPU:15, one launch (start us, length us, event | category | flops | bytes accessed | tf_op | source)
XLA Modules:
  0.0 1207.9 jit_solution(1366430794562868117)
XLA Ops:
  7.2 13.0 %shard_map.86 = bf16[256,32,512]{2,1,0:T(8,128)(2,1)} custom-call(bf16[32,512,512]{2,1,0:T(8,128)(2,1)} %bitcast.32), custom_call_target="tpu_custom_call" | custom-call | bytes 16777216 | tf_op jit(solution)/shard_map/pallas_call | solution.py:81
  20.2 6.6 all-to-all-start.2
  26.8 13.1 %shard_map.87 = bf16[256,32,512]{2,1,0:T(8,128)(2,1)} custom-call(bf16[32,512,512]{2,1,0:T(8,128)(2,1)} %bitcast.34), custom_call_target="tpu_custom_call" | custom-call | bytes 16777216 | tf_op jit(solution)/shard_map/pallas_call | solution.py:81
  39.8 169.3 %all-to-all-done.2.x_ref = bf16[16,16,32,512]{3,2,1,0:T(8,128)(2,1)} async-done(((bf16[16,16,32,512]{3,2,1,0:T(8,128)(2,1)}), bf16[16,16,32,512]{3,2,1,0:T(8,128)(2,1)}, u32[]{:S(2)}, u32[]{:S(2)}) %all-to-all-start.2) | async-done | bytes 8388640 | tf_op jit(solution)/shard_map/all_to_all | solution.py:138
  209.1 4.9 all-to-all-start.3
  214.0 13.0 %shard_map.84 = bf16[256,32,512]{2,1,0:T(8,128)(2,1)} custom-call(bf16[32,512,512]{2,1,0:T(8,128)(2,1)} %bitcast.33), custom_call_target="tpu_custom_call" | custom-call | bytes 16777216 | tf_op jit(solution)/shard_map/pallas_call | solution.py:81
  227.1 169.3 %all-to-all-done.3.dy_ref = bf16[16,16,32,512]{3,2,1,0:T(8,128)(2,1)} async-done(((bf16[16,16,32,512]{3,2,1,0:T(8,128)(2,1)}), bf16[16,16,32,512]{3,2,1,0:T(8,128)(2,1)}, u32[]{:S(2)}, u32[]{:S(2)}) %all-to-all-start.3) | async-done | bytes 8388640 | tf_op jit(solution)/shard_map/all_to_all | solution.py:138
  396.4 4.9 all-to-all-start
  401.3 13.1 %shard_map.85 = bf16[256,32,512]{2,1,0:T(8,128)(2,1)} custom-call(bf16[32,512,512]{2,1,0:T(8,128)(2,1)} %bitcast.35), custom_call_target="tpu_custom_call" | custom-call | bytes 16777216 | tf_op jit(solution)/shard_map/pallas_call | solution.py:81
  414.4 169.2 %all-to-all-done.x_ref = bf16[16,16,32,512]{3,2,1,0:T(8,128)(2,1)} async-done(((bf16[16,16,32,512]{3,2,1,0:T(8,128)(2,1)}), bf16[16,16,32,512]{3,2,1,0:T(8,128)(2,1)}, u32[]{:S(2)}, u32[]{:S(2)}) %all-to-all-start) | async-done | bytes 8388640 | tf_op jit(solution)/shard_map/all_to_all | solution.py:138
  583.6 0.0 copy-start.5
  583.6 5.0 all-to-all-start.1
  588.7 0.0 all-gather.3.cloned.1.call-start
  588.7 0.0 copy-done.5
  588.7 0.0 copy-done.6
  588.7 0.0 copy-done.4
  588.8 0.7 pad_maximum_fusion
  589.5 0.0 all-gather.3.cloned.1.call-update
  589.5 154.1 %all-gather.3.cloned.1.call-done = f32[48,32,512]{2,1,0:T(8,128)} async-done(((f32[3,32,512]{2,1,0:T(8,128)}), f32[48,32,512]{2,1,0:T(8,128)}) %all-gather.3.cloned.1.call-update) | async-done | bytes 3145744 | tf_op jit(solution)/shard_map/all_gather | solution.py:141
  743.6 2.1 convert.6
  745.7 1.3 slice.34
  747.0 0.1 fusion
  747.1 0.0 copy-start
  747.1 0.0 copy-start.1
  747.1 1.1 copy.27
  748.3 1.0 copy.28
  749.3 1.3 copy.29
  750.6 1.1 broadcast_in_dim.3.gf_in.gs_in.gt_in
  751.7 0.0 copy-done
  751.7 0.0 copy-done.1
  751.7 37.4 %shard_map.88 = (bf16[16,16,32,512]{3,2,1,0:T(8,128)(2,1)}, f32[512,512]{1,0:T(8,128)}, f32[512,512]{1,0:T(8,128)}, f32[512,512]{1,0:T(8,128)}) custom-call(bf16[16,16,32,512]{3,2,1,0:T(8,128)(2,1)} %all-to-all-done.2.x_ref, bf16[16,16,32,512]{3,2,1,0:T(8,128)(2,1)} %all-to-all-done.3.dy_ref, bf16[512,512]{1,0:T(8,128)(2,1)} %bitcast.50, ...), custom_call_target="tpu_custom_call" | custom-call | flops 25769803776 | bytes 33030144 | tf_op jit(solution)/shard_map/pallas_call | solution.py:50
  789.2 0.9 all-to-all-done.1.dy_ref
  790.0 10.3 all-to-all-start.5
  800.3 37.2 %shard_map.89 = (bf16[16,16,32,512]{3,2,1,0:T(8,128)(2,1)}, f32[512,512]{1,0:T(8,128)}, f32[512,512]{1,0:T(8,128)}, f32[512,512]{1,0:T(8,128)}) custom-call(bf16[16,16,32,512]{3,2,1,0:T(8,128)(2,1)} %all-to-all-done.x_ref, bf16[16,16,32,512]{3,2,1,0:T(8,128)(2,1)} %all-to-all-done.1.dy_ref, bf16[512,512]{1,0:T(8,128)(2,1)} %bitcast.51, ...), custom_call_target="tpu_custom_call" | custom-call | flops 25769803776 | bytes 33030144 | tf_op jit(solution)/shard_map/pallas_call | solution.py:50
  837.5 145.2 %all-to-all-done.5 = bf16[16,16,32,512]{3,2,1,0:T(8,128)(2,1)} async-done(((bf16[16,16,32,512]{3,2,1,0:T(8,128)(2,1)}), bf16[16,16,32,512]{3,2,1,0:T(8,128)(2,1)}, u32[]{:S(2)}, u32[]{:S(2)}) %all-to-all-start.5) | async-done | bytes 8388640 | tf_op jit(solution)/shard_map/all_to_all | solution.py:151
  982.7 5.0 all-to-all-start.4
  987.7 0.0 reduce-scatter.2.cloned.1.call-start
  987.7 0.0 copy-done.2
  987.7 0.3 copy.30
  988.1 0.0 copy-done.3
  988.1 1.5 maximum_bitcast_fusion
  989.6 2.0 copy.31
  991.6 0.0 reduce-scatter.2.cloned.1.call-update
  991.6 158.4 %reduce-scatter.2.cloned.1.call-done = f32[96,512]{1,0:T(8,128)} async-done(((f32[1536,512]{1,0:T(8,128)}), f32[96,512]{1,0:T(8,128)}) %reduce-scatter.2.cloned.1.call-update) | async-done | bytes 196624 | tf_op jit(solution)/shard_map/reduce_scatter | solution.py:157
  1150.0 1.6 slice_multiply_fusion
  1151.6 12.1 %shard_map.90.refs_0_ = bf16[32,512,512]{2,1,0:T(8,128)(2,1)} custom-call(bf16[256,32,512]{2,1,0:T(8,128)(2,1)} %bitcast.19.b_ref), custom_call_target="tpu_custom_call" | custom-call | bytes 16777216 | tf_op jit(solution)/shard_map/pallas_call | solution.py:111
  1163.7 25.3 %all-to-all-done.4 = bf16[16,16,32,512]{3,2,1,0:T(8,128)(2,1)} async-done(((bf16[16,16,32,512]{3,2,1,0:T(8,128)(2,1)}), bf16[16,16,32,512]{3,2,1,0:T(8,128)(2,1)}, u32[]{:S(2)}, u32[]{:S(2)}) %all-to-all-start.4) | async-done | bytes 8388640 | tf_op jit(solution)/shard_map/all_to_all | solution.py:151
  1189.0 12.1 %shard_map.91 = bf16[32,512,512]{2,1,0:T(8,128)(2,1)} custom-call(bf16[256,32,512]{2,1,0:T(8,128)(2,1)} %bitcast.18.b_ref, bf16[32,512,512]{2,1,0:T(8,128)(2,1)} %shard_map.90.refs_0_), custom_call_target="tpu_custom_call", output_to_operand_aliasing={{}: (1, {})} | custom-call | bytes 16777216 | tf_op jit(solution)/shard_map/pallas_call | solution.py:111
  (5 shorter events, 0.0 us)
Async XLA Ops:
  20.2 188.9 %all-to-all-start.2 = ((bf16[16,16,32,512]{3,2,1,0:T(8,128)(2,1)}), bf16[16,16,32,512]{3,2,1,0:T(8,128)(2,1)}, u32[]{:S(2)}, u32[]{:S(2)}) async-start(bf16[16,16,32,512]{3,2,1,0:T(8,128)(2,1)} %bitcast.40), calls=%async_computation.2 | async-start | bytes 16777216 | tf_op jit(solution)/shard_map/all_to_all | solution.py:138
  209.1 187.3 %all-to-all-start.3 = ((bf16[16,16,32,512]{3,2,1,0:T(8,128)(2,1)}), bf16[16,16,32,512]{3,2,1,0:T(8,128)(2,1)}, u32[]{:S(2)}, u32[]{:S(2)}) async-start(bf16[16,16,32,512]{3,2,1,0:T(8,128)(2,1)} %bitcast.38), calls=%async_computation.3 | async-start | bytes 16777216 | tf_op jit(solution)/shard_map/all_to_all | solution.py:138
  396.4 187.3 %all-to-all-start = ((bf16[16,16,32,512]{3,2,1,0:T(8,128)(2,1)}), bf16[16,16,32,512]{3,2,1,0:T(8,128)(2,1)}, u32[]{:S(2)}, u32[]{:S(2)}) async-start(bf16[16,16,32,512]{3,2,1,0:T(8,128)(2,1)} %bitcast.39), calls=%async_computation | async-start | bytes 16777216 | tf_op jit(solution)/shard_map/all_to_all | solution.py:138
  583.6 5.1 copy-start.5
  583.6 5.1 copy-start.6
  583.6 5.1 copy-start.4
  583.6 206.4 %all-to-all-start.1 = ((bf16[16,16,32,512]{3,2,1,0:T(8,128)(2,1)}), bf16[16,16,32,512]{3,2,1,0:T(8,128)(2,1)}, u32[]{:S(2)}, u32[]{:S(2)}) async-start(bf16[16,16,32,512]{3,2,1,0:T(8,128)(2,1)} %bitcast.37), calls=%async_computation.1 | async-start | bytes 16777216 | tf_op jit(solution)/shard_map/all_to_all | solution.py:138
  588.7 154.9 %all-gather.3.cloned.1.call-start = ((), (), s32[]{:S(2)}) async-start(), calls=%async_computation.8 | async-start | bytes 3342336 | tf_op jit(solution)/shard_map/all_gather | solution.py:141
  747.1 4.6 copy-start
  747.1 4.6 copy-start.1
  790.0 192.6 %all-to-all-start.5 = ((bf16[16,16,32,512]{3,2,1,0:T(8,128)(2,1)}), bf16[16,16,32,512]{3,2,1,0:T(8,128)(2,1)}, u32[]{:S(2)}, u32[]{:S(2)}) async-start(bf16[16,16,32,512]{3,2,1,0:T(8,128)(2,1)} %get-tuple-element.16), calls=%async_computation.5 | async-start | bytes 16777216 | tf_op jit(solution)/shard_map/all_to_all | solution.py:151
  982.6 5.1 copy-start.2
  982.6 5.4 copy-start.3
  982.7 206.3 %all-to-all-start.4 = ((bf16[16,16,32,512]{3,2,1,0:T(8,128)(2,1)}), bf16[16,16,32,512]{3,2,1,0:T(8,128)(2,1)}, u32[]{:S(2)}, u32[]{:S(2)}) async-start(bf16[16,16,32,512]{3,2,1,0:T(8,128)(2,1)} %get-tuple-element.15), calls=%async_computation.4 | async-start | bytes 16777216 | tf_op jit(solution)/shard_map/all_to_all | solution.py:151
  987.7 162.3 %reduce-scatter.2.cloned.1.call-start = ((), (), s32[]{:S(2)}) async-start(), calls=%async_computation.7 | async-start | bytes 3342336 | tf_op jit(solution)/shard_map/reduce_scatter | solution.py:157
Sparse Core Ops, SparseCore 0:
  592.4 151.1 all-gather.2
  992.9 157.0 reduce-scatter.1

commit v2 on v1

--- a/solution.py
+++ b/solution.py
@@ -63,7 +63,8 @@
     return gi, tuple(grads)
 
 
-def to_channels_kernel(x_ref, o_ref, held):
+def to_channels_kernel(x_ref, *refs):
+    o_ref, held = refs[-2:]
     count = x_ref.shape[0]
     lanes = x_ref.shape[2]
     for i in range(count):
@@ -75,21 +76,22 @@
         o_ref[:, :, pl.ds(q * LANES, LANES)] = piece.reshape(lanes, count, LANES).astype(BF16)
 
 
-def to_channels(array, at, chunk):
+def to_channels(array, at, chunk, after):
     rows, order, _ = array.shape
     count = min(rows, 16)
     return pl.pallas_call(
         to_channels_kernel,
         grid=(chunk // LANES, rows // count),
         out_shape=jax.ShapeDtypeStruct((chunk, rows, order), BF16),
-        in_specs=[pl.BlockSpec((count, order, LANES), lambda c, i: (i, 0, at // LANES + c))],
+        in_specs=[pl.BlockSpec((count, order, LANES), lambda c, i: (i, 0, at // LANES + c))]
+        + [pl.BlockSpec(memory_space=pl.ANY)] * len(after),
         out_specs=pl.BlockSpec((LANES, count, order), lambda c, i: (c, i, 0)),
         scratch_shapes=[pltpu.VMEM((count * order, LANES), F32)],
         compiler_params=pltpu.CompilerParams(vmem_limit_bytes=56 * 1024 * 1024),
         cost_estimate=pl.CostEstimate(
             flops=0, bytes_accessed=4 * chunk * rows * order, transcendentals=0
         ),
-    )(array)
+    )(array, *after)
 
 
 def to_positions_kernel(b_ref, *refs):
@@ -133,8 +135,8 @@
     xval = inputs.reshape(rows, order, channels)
     dyval = cotangent.reshape(rows, order, channels)
 
-    def send(array, at):
-        part = to_channels(array, at, chunk).reshape(devices, own, rows, order)
+    def send(array, at, *after):
+        part = to_channels(array, at, chunk, after).reshape(devices, own, rows, order)
         return lax.all_to_all(part, "seq", split_axis=0, concat_axis=0)
 
     small = jnp.stack([first_block.astype(F32), second_block.astype(F32), twiddle])
@@ -146,8 +148,11 @@
     zero = jnp.zeros((order, order), F32)
     grads = (zero, zero, zero)
     result = ()
+    before = small
     for at in range(0, channels, chunk):
-        gi, grads = channels_call(send(xval, at), send(dyval, at), f, ft, s, st, tw, grads)
+        xc, dyc = send(xval, at), send(dyval, at, before)
+        gi, grads = channels_call(xc, dyc, f, ft, s, st, tw, grads)
+        before = gi
         back = lax.all_to_all(gi, "seq", split_axis=0, concat_axis=0)
         result = (to_positions(back.reshape(chunk, rows, order), at, channels, result),)
 

time: 1210 us -> 1200 us (level)
  blocking collectives: 0 us -> 187 us
  waiting for transfers between devices: 992 us -> 806 us
    all_to_all x0 -> x1, blocking collectives: none -> 187 us  [send(): return lax.all_to_all(part, 'seq', split_axis=0, concat_axis=0)]
    all_to_all x4 -> x3, waiting for transfers between devices: 509 us -> 323 us  [send(): return lax.all_to_all(part, 'seq', split_axis=0, concat_axis=0)]
    all_to_all x2, waiting for transfers between devices: 170 us -> 193 us  [on_device(): back = lax.all_to_all(gi, 'seq', split_axis=0, concat_axis=0)]
    reduce_scatter x1, waiting for transfers between devices: 158 us -> 136 us  [on_device(): terms = lax.psum_scatter(terms, 'seq', scatter_dimension=0, tiled=True)]
  transfers between devices with their start and end apart: 8 -> 7, of which waited for: 8 -> 7; matrix products, arithmetic and copies ran while one was open for 1% -> 1% of each run, Pallas kernels for 10% -> 10%
where the time goes in v2:
time: 1200 us
  waiting for transfers between devices  806 us (67%)
  blocking collectives  187 us (16%)
  Pallas kernels  151 us (13%)
  starting transfers between devices  27.5 us (2%)
  between operations  14.2 us (1%)
  local copies, waits for them, and re-layouts  13.4 us (1%)
    all_to_all x3, waiting for transfers between devices, send(): return lax.all_to_all(part, 'seq', split_axis=0, concat_axis=0)  323 us
    all_to_all x2, waiting for transfers between devices, on_device(): back = lax.all_to_all(gi, 'seq', split_axis=0, concat_axis=0)  193 us
    all_to_all x1, blocking collectives, send(): return lax.all_to_all(part, 'seq', split_axis=0, concat_axis=0)  187 us
    all_gather x1, waiting for transfers between devices, on_device(): small = lax.all_gather(small, 'seq', axis=0)  154 us
    reduce_scatter x1, waiting for transfers between devices, on_device(): terms = lax.psum_scatter(terms, 'seq', scatter_dimension=0, tiled=True)  136 us
    pallas_call x2, Pallas kernels, channels_call(): pl.pallas_call(channel_kernel, grid=(own,), out_shape=(jax.ShapeDtypeStru...  74.6 us
    pallas_call x4, Pallas kernels, to_channels(): pl.pallas_call(to_channels_kernel, grid=(chunk // LANES, rows // count),...  52.3 us
    pallas_call x2, Pallas kernels, to_positions(): pl.pallas_call(to_positions_kernel, grid=(chunk // LANES, rows // count),...  24.2 us
  transfers between devices with their start and end apart: 7, of which 7 were waited for; matrix products, arithmetic and copies ran while one was open for 1% of the time, Pallas kernels for 10%

profile of v2, /device:TPU:15, one launch (start us, length us, event | category | flops | bytes accessed | tf_op | source)
XLA Modules:
  0.0 1203.5 jit_solution(8190258528157129865)
XLA Ops:
  7.2 13.0 %shard_map.85 = bf16[256,32,512]{2,1,0:T(8,128)(2,1)} custom-call(bf16[32,512,512]{2,1,0:T(8,128)(2,1)} %bitcast.33), custom_call_target="tpu_custom_call" | custom-call | bytes 16777216 | tf_op jit(solution)/shard_map/pallas_call | solution.py:82
  20.2 6.7 all-to-all-start.1
  26.9 0.0 all-gather.3.cloned.1.call-start
  26.9 0.0 copy-done.6
  27.0 0.0 copy-done.7
  27.0 0.0 copy-done.5
  27.0 0.7 pad_maximum_fusion
  27.7 0.0 all-gather.3.cloned.1.call-update
  27.7 154.1 %all-gather.3.cloned.1.call-done = f32[48,32,512]{2,1,0:T(8,128)} async-done(((f32[3,32,512]{2,1,0:T(8,128)}), f32[48,32,512]{2,1,0:T(8,128)}) %all-gather.3.cloned.1.call-update) | async-done | bytes 3145744 | tf_op jit(solution)/shard_map/all_gather | solution.py:143
  181.8 4.1 copy.29
  185.9 13.1 %shard_map.86 = bf16[256,32,512]{2,1,0:T(8,128)(2,1)} custom-call(bf16[32,512,512]{2,1,0:T(8,128)(2,1)} %bitcast.35, f32[3,512,512]{2,1,0:T(8,128)} %bitcast.45), custom_call_target="tpu_custom_call" | custom-call | bytes 16777216 | tf_op jit(solution)/shard_map/pallas_call | solution.py:82
  199.0 29.2 %all-to-all-done.1.x_ref = bf16[16,16,32,512]{3,2,1,0:T(8,128)(2,1)} async-done(((bf16[16,16,32,512]{3,2,1,0:T(8,128)(2,1)}), bf16[16,16,32,512]{3,2,1,0:T(8,128)(2,1)}, u32[]{:S(2)}, u32[]{:S(2)}) %all-to-all-start.1) | async-done | bytes 8388640 | tf_op jit(solution)/shard_map/all_to_all | solution.py:140
  228.2 4.8 all-to-all-start.2
  233.1 13.0 %shard_map.84 = bf16[256,32,512]{2,1,0:T(8,128)(2,1)} custom-call(bf16[32,512,512]{2,1,0:T(8,128)(2,1)} %bitcast.34), custom_call_target="tpu_custom_call" | custom-call | bytes 16777216 | tf_op jit(solution)/shard_map/pallas_call | solution.py:82
  246.1 169.3 %all-to-all-done.2.dy_ref = bf16[16,16,32,512]{3,2,1,0:T(8,128)(2,1)} async-done(((bf16[16,16,32,512]{3,2,1,0:T(8,128)(2,1)}), bf16[16,16,32,512]{3,2,1,0:T(8,128)(2,1)}, u32[]{:S(2)}, u32[]{:S(2)}) %all-to-all-start.2) | async-done | bytes 8388640 | tf_op jit(solution)/shard_map/all_to_all | solution.py:140
  415.4 5.2 all-to-all-start
  420.6 0.0 copy-done
  420.6 0.2 convert.6
  420.9 1.1 slice.34
  422.0 0.1 fusion
  422.1 0.0 copy-start.1
  422.1 0.0 copy-start.2
  422.1 1.1 copy.30
  423.2 1.0 copy.31
  424.2 2.5 copy.32
  426.8 1.1 broadcast_in_dim.3.gf_in.gs_in.gt_in
  427.9 0.0 copy-done.1
  427.9 0.0 copy-done.2
  427.9 37.4 %shard_map.87 = (bf16[16,16,32,512]{3,2,1,0:T(8,128)(2,1)}, f32[512,512]{1,0:T(8,128)}, f32[512,512]{1,0:T(8,128)}, f32[512,512]{1,0:T(8,128)}) custom-call(bf16[16,16,32,512]{3,2,1,0:T(8,128)(2,1)} %all-to-all-done.1.x_ref, bf16[16,16,32,512]{3,2,1,0:T(8,128)(2,1)} %all-to-all-done.2.dy_ref, bf16[512,512]{1,0:T(8,128)(2,1)} %bitcast.53, ...), custom_call_target="tpu_custom_call" | custom-call | flops 25769803776 | bytes 33030144 | tf_op jit(solution)/shard_map/pallas_call | solution.py:50
  465.3 13.1 %shard_map.88 = bf16[256,32,512]{2,1,0:T(8,128)(2,1)} custom-call(bf16[32,512,512]{2,1,0:T(8,128)(2,1)} %bitcast.36, bf16[16,16,32,512]{3,2,1,0:T(8,128)(2,1)} %get-tuple-element.12.refs_0_), custom_call_target="tpu_custom_call" | custom-call | bytes 16777216 | tf_op jit(solution)/shard_map/pallas_call | solution.py:82
  478.4 124.5 %all-to-all-done.x_ref = bf16[16,16,32,512]{3,2,1,0:T(8,128)(2,1)} async-done(((bf16[16,16,32,512]{3,2,1,0:T(8,128)(2,1)}), bf16[16,16,32,512]{3,2,1,0:T(8,128)(2,1)}, u32[]{:S(2)}, u32[]{:S(2)}) %all-to-all-start) | async-done | bytes 8388640 | tf_op jit(solution)/shard_map/all_to_all | solution.py:140
  602.9 187.1 %all_to_all.30.dy_ref = bf16[16,16,32,512]{3,2,1,0:T(8,128)(2,1)} all-to-all(bf16[16,16,32,512]{3,2,1,0:T(8,128)(2,1)} %bitcast.41), channel_id=1, replica_groups=mesh['parts'=2,'seq'=16] {'seq'}, dimensions={0} | all-to-all | bytes 16777216 | tf_op jit(solution)/shard_map/all_to_all | solution.py:140
  790.1 5.7 all-to-all-start.5
  795.8 37.2 %shard_map.89 = (bf16[16,16,32,512]{3,2,1,0:T(8,128)(2,1)}, f32[512,512]{1,0:T(8,128)}, f32[512,512]{1,0:T(8,128)}, f32[512,512]{1,0:T(8,128)}) custom-call(bf16[16,16,32,512]{3,2,1,0:T(8,128)(2,1)} %all-to-all-done.x_ref, bf16[16,16,32,512]{3,2,1,0:T(8,128)(2,1)} %all_to_all.30.dy_ref, bf16[512,512]{1,0:T(8,128)(2,1)} %bitcast.54, ...), custom_call_target="tpu_custom_call" | custom-call | flops 25769803776 | bytes 33030144 | tf_op jit(solution)/shard_map/pallas_call | solution.py:50
  833.0 145.2 %all-to-all-done.5 = bf16[16,16,32,512]{3,2,1,0:T(8,128)(2,1)} async-done(((bf16[16,16,32,512]{3,2,1,0:T(8,128)(2,1)}), bf16[16,16,32,512]{3,2,1,0:T(8,128)(2,1)}, u32[]{:S(2)}, u32[]{:S(2)}) %all-to-all-start.5) | async-done | bytes 8388640 | tf_op jit(solution)/shard_map/all_to_all | solution.py:156
  978.1 5.0 all-to-all-start.4
  983.2 0.0 reduce-scatter.2.cloned.1.call-start
  983.2 0.0 copy-done.3
  983.2 0.3 copy.33
  983.6 0.0 copy-done.4
  983.6 1.5 maximum_bitcast_fusion
  985.1 1.9 copy.34
  987.0 0.0 reduce-scatter.2.cloned.1.call-update
  987.1 12.1 %shard_map.90.refs_0_ = bf16[32,512,512]{2,1,0:T(8,128)(2,1)} custom-call(bf16[256,32,512]{2,1,0:T(8,128)(2,1)} %bitcast.20.b_ref), custom_call_target="tpu_custom_call" | custom-call | bytes 16777216 | tf_op jit(solution)/shard_map/pallas_call | solution.py:113
  999.2 135.7 %reduce-scatter.2.cloned.1.call-done = f32[96,512]{1,0:T(8,128)} async-done(((f32[1536,512]{1,0:T(8,128)}), f32[96,512]{1,0:T(8,128)}) %reduce-scatter.2.cloned.1.call-update) | async-done | bytes 196624 | tf_op jit(solution)/shard_map/reduce_scatter | solution.py:162
  1134.9 1.6 slice_multiply_fusion
  1136.4 48.1 %all-to-all-done.4 = bf16[16,16,32,512]{3,2,1,0:T(8,128)(2,1)} async-done(((bf16[16,16,32,512]{3,2,1,0:T(8,128)(2,1)}), bf16[16,16,32,512]{3,2,1,0:T(8,128)(2,1)}, u32[]{:S(2)}, u32[]{:S(2)}) %all-to-all-start.4) | async-done | bytes 8388640 | tf_op jit(solution)/shard_map/all_to_all | solution.py:156
  1184.5 12.1 %shard_map.91 = bf16[32,512,512]{2,1,0:T(8,128)(2,1)} custom-call(bf16[256,32,512]{2,1,0:T(8,128)(2,1)} %bitcast.19.b_ref, bf16[32,512,512]{2,1,0:T(8,128)(2,1)} %shard_map.90.refs_0_), custom_call_target="tpu_custom_call", output_to_operand_aliasing={{}: (1, {})} | custom-call | bytes 16777216 | tf_op jit(solution)/shard_map/pallas_call | solution.py:113
  (7 shorter events, 0.0 us)
Async XLA Ops:
  20.2 6.7 copy-start.6
  20.2 6.8 copy-start.7
  20.2 6.8 copy-start.5
  20.2 208.0 %all-to-all-start.1 = ((bf16[16,16,32,512]{3,2,1,0:T(8,128)(2,1)}), bf16[16,16,32,512]{3,2,1,0:T(8,128)(2,1)}, u32[]{:S(2)}, u32[]{:S(2)}) async-start(bf16[16,16,32,512]{3,2,1,0:T(8,128)(2,1)} %bitcast.39), calls=%async_computation.1 | async-start | bytes 16777216 | tf_op jit(solution)/shard_map/all_to_all | solution.py:140
  26.9 154.9 %all-gather.3.cloned.1.call-start = ((), (), s32[]{:S(2)}) async-start(), calls=%async_computation.8 | async-start | bytes 3342336 | tf_op jit(solution)/shard_map/all_gather | solution.py:143
  228.2 187.2 %all-to-all-start.2 = ((bf16[16,16,32,512]{3,2,1,0:T(8,128)(2,1)}), bf16[16,16,32,512]{3,2,1,0:T(8,128)(2,1)}, u32[]{:S(2)}, u32[]{:S(2)}) async-start(bf16[16,16,32,512]{3,2,1,0:T(8,128)(2,1)} %bitcast.40), calls=%async_computation.2 | async-start | bytes 16777216 | tf_op jit(solution)/shard_map/all_to_all | solution.py:140
  415.4 5.2 copy-start
  415.4 187.5 %all-to-all-start = ((bf16[16,16,32,512]{3,2,1,0:T(8,128)(2,1)}), bf16[16,16,32,512]{3,2,1,0:T(8,128)(2,1)}, u32[]{:S(2)}, u32[]{:S(2)}) async-start(bf16[16,16,32,512]{3,2,1,0:T(8,128)(2,1)} %bitcast.38), calls=%async_computation | async-start | bytes 16777216 | tf_op jit(solution)/shard_map/all_to_all | solution.py:140
  422.1 5.8 copy-start.1
  422.1 5.8 copy-start.2
  790.1 188.0 %all-to-all-start.5 = ((bf16[16,16,32,512]{3,2,1,0:T(8,128)(2,1)}), bf16[16,16,32,512]{3,2,1,0:T(8,128)(2,1)}, u32[]{:S(2)}, u32[]{:S(2)}) async-start(bf16[16,16,32,512]{3,2,1,0:T(8,128)(2,1)} %get-tuple-element.12.refs_0_), calls=%async_computation.5 | async-start | bytes 16777216 | tf_op jit(solution)/shard_map/all_to_all | solution.py:156
  978.1 5.1 copy-start.3
  978.1 5.4 copy-start.4
  978.1 206.4 %all-to-all-start.4 = ((bf16[16,16,32,512]{3,2,1,0:T(8,128)(2,1)}), bf16[16,16,32,512]{3,2,1,0:T(8,128)(2,1)}, u32[]{:S(2)}, u32[]{:S(2)}) async-start(bf16[16,16,32,512]{3,2,1,0:T(8,128)(2,1)} %get-tuple-element.16), calls=%async_computation.4 | async-start | bytes 16777216 | tf_op jit(solution)/shard_map/all_to_all | solution.py:156
  983.2 151.7 %reduce-scatter.2.cloned.1.call-start = ((), (), s32[]{:S(2)}) async-start(), calls=%async_computation.7 | async-start | bytes 3342336 | tf_op jit(solution)/shard_map/reduce_scatter | solution.py:162
Sparse Core Ops, SparseCore 0:
  30.0 151.7 all-gather.2
  987.8 146.9 reduce-scatter.1
